TPU v7x, 256 devices: a whole 4x4x8 slice. The times are simulated.
256 devices in a mesh: blk: 16 (over y, x_hi, core), seq: 16 (over z, x_lo).
Axes of the slice: x: 4 (x_hi: 2, x_lo: 2; x = x_hi * 2 + x_lo), y: 4, z: 8, core: 2. Of those that a mesh axis runs over, the one named last changes fastest.
Arguments:
- saved_input: bfloat16 [16, 2048, 8192], P('blk', 'seq'), may hold values from -180 to 180
- output_grad: bfloat16 [16, 2048, 8192], P('blk', 'seq'), may hold values from -0.3984375 to 0.3984375
- weight_span: bfloat16 [16, 8192, 3, 256], P('blk', 'seq'), may hold values from -0.0625 to 0.0625
- grad_carry: float32 [16, 8192, 3, 256], P('blk', 'seq'), may hold values from -6 to 6
- attn_queries: bfloat16 [16, 2048, 4096], P('blk', 'seq'), may hold values from -6 to 6
- attn_keys: bfloat16 [16, 2048, 512], P('blk', 'seq'), may hold values from -6 to 6
- attn_values: bfloat16 [16, 2048, 512], P('blk', 'seq'), may hold values from -6 to 6
Outputs:
- carry_out: float32 [16, 8192, 3, 256], P('blk', 'seq')
- attn_out: bfloat16 [16, 2048, 4096], P('blk', 'seq')
All inputs are finite; a program needn't handle non-finite values.
Results may differ from a plain program's by a relative error of at most 0.02.
Values may be sent and summed in bfloat16 or wider, within the bound.
No kernel may reach another device: no remote copies, remote signals or barrier semaphores. Data moves between devices by JAX's collectives and lax.ppermute only.
A program may use at most 192 MiB of HBM per device.

v0:
```python
import jax
import jax.numpy as jnp
from jax import lax
from jax.sharding import PartitionSpec as P

HD = 128
QH = 32
KVH = 4


EPSILON = 1e-05
NEGATIVE = -1e30


def shifted(block, axis, distance):
    devices = range(lax.axis_size(axis))
    route = [((i - distance) % len(devices), i) for i in devices]
    return lax.ppermute(block, axis, route)


def matmul(left, right):
    return jnp.dot(left, right, preferred_element_type=jnp.float32)


def token_contract(left, right):
    return lax.dot_general(
        left, right, (((0,), (0,)), ((), ())), preferred_element_type=jnp.float32
    )


def normalize(activation):
    widened = activation.astype(jnp.float32)
    factor = lax.rsqrt(jnp.mean(widened * widened, axis=-1, keepdims=True) + EPSILON)
    return (widened * factor).astype(jnp.bfloat16)


def swiglu_back(gate_sum, up_sum, hidden_grad):
    sigmoid_gate = jax.nn.sigmoid(gate_sum)
    activated = gate_sum * sigmoid_gate
    hidden = (activated * up_sum).astype(jnp.bfloat16)
    up_grad = (hidden_grad * activated).astype(jnp.bfloat16)
    gate_grad = (
        hidden_grad * up_sum * sigmoid_gate * (1.0 + gate_sum * (1.0 - sigmoid_gate))
    ).astype(jnp.bfloat16)
    return (hidden, gate_grad, up_grad)


def shards(saved_input, output_grad, weight_span, grad_carry, attn_queries, attn_keys, attn_values):
    arrived = shifted(weight_span, "blk", 1)
    onward = shifted(grad_carry.astype(jnp.bfloat16), "blk", -1).astype(grad_carry.dtype)
    normed = normalize(saved_input[0])
    cotangent = output_grad[0]
    weights = arrived[0]
    shard_piece = lax.all_gather(weights, "seq", axis=0, tiled=True)
    normed_part = normed
    grad_part = cotangent
    gate_sum = matmul(normed_part, shard_piece[:, 0])
    up_sum = matmul(normed_part, shard_piece[:, 1])
    hidden_grad = matmul(grad_part, shard_piece[:, 2])
    hidden, gate_grad, up_grad = swiglu_back(gate_sum, up_sum, hidden_grad)
    normed_part = normed
    grad_part = cotangent
    update = lax.psum_scatter(
        jnp.stack(
            [
                token_contract(normed_part, gate_grad),
                token_contract(normed_part, up_grad),
                token_contract(grad_part, hidden),
            ],
            axis=1,
        ).astype(jnp.bfloat16),
        "seq",
        scatter_dimension=0,
        tiled=True,
    ).astype(jnp.float32)
    carry_out = (onward[0] + update)[None]
    queries = attn_queries[0]
    query_rows = queries.shape[0]
    group_size = QH // KVH
    grouped = queries.reshape(query_rows, KVH, group_size, HD)
    query_pos = lax.axis_index("seq") * query_rows + jnp.arange(query_rows, dtype=jnp.int32)
    first_row = jnp.int32(0)
    running_max = jnp.full((KVH, group_size, query_rows), NEGATIVE, jnp.float32)
    running_sum = jnp.zeros((KVH, group_size, query_rows), jnp.float32)
    summed = jnp.zeros((KVH, group_size, query_rows, HD), jnp.float32)
    key_piece = lax.all_gather(attn_keys[0], "seq", axis=0, tiled=True)
    value_piece = lax.all_gather(attn_values[0], "seq", axis=0, tiled=True)
    piece_rows = key_piece.shape[0]
    block_size = min(512, piece_rows)
    for offset in range(0, piece_rows, block_size):
        block_rows = min(block_size, piece_rows - offset)
        key_block = key_piece[offset : offset + block_rows].reshape(block_rows, KVH, HD)
        value_block = value_piece[offset : offset + block_rows].reshape(block_rows, KVH, HD)
        scores = jnp.einsum(
            "skgd,pkd->kgsp", grouped, key_block, preferred_element_type=jnp.float32
        ) * HD ** (-0.5)
        key_pos = first_row + offset + jnp.arange(block_rows, dtype=jnp.int32)
        allowed = key_pos[None, :] <= query_pos[:, None]
        scores = jnp.where(allowed, scores, NEGATIVE)
        new_max = jnp.maximum(running_max, jnp.max(scores, axis=-1))
        probs = jnp.where(allowed, jnp.exp(scores - new_max[..., None]), 0.0)
        rescale = jnp.exp(running_max - new_max)
        running_sum = running_sum * rescale + jnp.sum(probs, axis=-1)
        summed = summed * rescale[..., None] + jnp.einsum(
            "kgsp,pkd->kgsd",
            probs.astype(jnp.bfloat16),
            value_block,
            preferred_element_type=jnp.float32,
        )
        running_max = new_max
    running_max, running_sum, summed = (running_max, running_sum, summed)
    result = summed / running_sum[..., None]
    attn_out = (
        jnp.transpose(result, (2, 0, 1, 3)).reshape(query_rows, QH * HD).astype(jnp.bfloat16)[None]
    )
    return (carry_out, attn_out)


def solution(mesh):
    return jax.shard_map(
        shards,
        mesh=mesh,
        in_specs=(
            P("blk", "seq", None),
            P("blk", "seq", None),
            P("blk", "seq", None, None),
            P("blk", "seq", None, None),
            P("blk", "seq", None),
            P("blk", "seq", None),
            P("blk", "seq", None),
        ),
        out_specs=(P("blk", "seq", None, None), P("blk", "seq", None)),
        check_vma=False,
    )
```

profile of v0, /device:TPU:1, one launch (start us, length us, event | category | flops | bytes accessed | tf_op | source)
XLA Modules:
  0.0 733.0 jit_solution(13961923744805023772)
XLA Ops:
  7.2 4.2 collective-permute-start.1
  11.4 9.3 %collective-permute-done.1 = bf16[1,512,3,256]{3,1,2,0:T(8,128)(2,1)S(1)} collective-permute-done((bf16[1,512,3,256]{3,1,2,0:T(8,128)(2,1)}, bf16[1,512,3,256]{3,1,2,0:T(8,128)(2,1)S(1)}, u32[]{:S(2)}, u32[]{:S(2)}) %collective-permute-start.1) | collective-permute-done | bytes 786464 | tf_op jit(solution)/shard_map/ppermute | solution.py:18
  22.4 1.7 copy.24
  24.1 2.1 fusion.17
  26.2 265.8 %all-gather.7.cloned.1.call-done = bf16[1,8192,3,256]{3,1,2,0:T(8,128)(2,1)} async-done(((bf16[1,512,3,256]{3,1,2,0:T(8,128)(2,1)}), bf16[1,8192,3,256]{3,1,2,0:T(8,128)(2,1)}) %all-gather.7.cloned.1.call-update) | async-done | bytes 12582928 | tf_op jit(solution)/shard_map/all_gather | solution.py:54
  292.0 3.7 fusion.20
  295.7 3.0 fusion.21
  300.1 2.9 fusion.22
  305.7 5.4 pad_maximum_fusion
  316.6 45.0 %all-gather.11.cloned.1.call-done = bf16[1,2048,512]{2,1,0:T(8,128)(2,1)} async-done(((bf16[1,128,512]{2,1,0:T(8,128)(2,1)}), bf16[1,2048,512]{2,1,0:T(8,128)(2,1)}) %all-gather.11.cloned.1.call-update) | async-done | bytes 2097168 | tf_op jit(solution)/shard_map/all_gather | solution.py:87
  367.3 76.6 %all-gather.9.cloned.1.call-done = bf16[1,2048,512]{1,2,0:T(8,128)(2,1)} async-done(((bf16[1,128,512]{1,2,0:T(8,128)(2,1)}), bf16[1,2048,512]{1,2,0:T(8,128)(2,1)}) %all-gather.9.cloned.1.call-update) | async-done | bytes 2097168 | tf_op jit(solution)/shard_map/all_gather | solution.py:86
  443.9 1.7 fusion.89
  445.5 3.0 fusion.6
  448.5 2.1 fusion.5
  450.6 2.1 fusion.4
  452.7 2.1 fusion.3
  454.8 4.8 fusion.7
  459.6 4.5 fusion.11
  464.1 3.5 fusion.23
  467.6 2.2 fusion.25
  469.8 2.2 fusion.27
  472.0 2.8 fusion.37
  476.1 247.7 %reduce-scatter.2.cloned.1.call-done = bf16[512,3,256]{2,0,1:T(8,128)(2,1)} async-done(((bf16[8192,3,256]{2,0,1:T(8,128)(2,1)}), bf16[512,3,256]{2,0,1:T(8,128)(2,1)}) %reduce-scatter.2.cloned.1.call-update) | async-done | bytes 786448 | tf_op jit(solution)/shard_map/reduce_scatter | solution.py:63
  723.8 2.7 fusion.45
  (53 shorter events, 18.3 us)
Async XLA Ops:
  7.2 291.6 %copy-start = (bf16[1,128,8192]{2,1,0:T(8,128)(2,1)S(1)}, bf16[1,128,8192]{2,1,0:T(8,128)(2,1)}, u32[]{:S(2)}) copy-start(bf16[1,128,8192]{2,1,0:T(8,128)(2,1)} %param.8) | copy-start | bytes 6291460
  7.2 284.8 %all-gather.7.cloned.1.call-start = ((), (), s32[]{:S(2)}) async-start(), calls=%async_computation.2 | async-start | bytes 13369344 | tf_op jit(solution)/shard_map/all_gather | solution.py:54
  7.2 13.5 %collective-permute-start.1 = (bf16[1,512,3,256]{3,1,2,0:T(8,128)(2,1)}, bf16[1,512,3,256]{3,1,2,0:T(8,128)(2,1)S(1)}, u32[]{:S(2)}, u32[]{:S(2)}) collective-permute-start(bf16[1,512,3,256]{3,1,2,0:T(8,128)(2,1)} %param.9), channel_id=1, source_target_pairs={{240,0},{0,16},{16,32},{32,48},{48,64},{64,80},{80,96},{96,112},{1... | collective-permute-start | bytes 2359304 | tf_op jit(solution)/shard_map/ppermute | solution.py:18
  20.7 0.9 copy-start.6
  21.6 340.0 %all-gather.11.cloned.1.call-start = ((), (), s32[]{:S(2)}) async-start(), calls=%async_computation.4 | async-start | bytes 2228224 | tf_op jit(solution)/shard_map/all_gather | solution.py:87
  22.3 421.5 %all-gather.9.cloned.1.call-start = ((), (), s32[]{:S(2)}) async-start(), calls=%async_computation.3 | async-start | bytes 2228224 | tf_op jit(solution)/shard_map/all_gather | solution.py:86
  24.1 699.7 %reduce-scatter.2.cloned.1.call-start = ((), (), s32[]{:S(2)}) async-start(), calls=%async_computation.1 | async-start | bytes 13369344 | tf_op jit(solution)/shard_map/reduce_scatter | solution.py:63
  292.0 3.7 copy-start.2
  311.2 1.4 copy-start.3
  313.5 162.6 %collective-permute-start = (bf16[1,512,3,256]{3,1,2,0:T(8,128)(2,1)}, bf16[1,512,3,256]{3,1,2,0:T(8,128)(2,1)}, u32[]{:S(2)}, u32[]{:S(2)}) collective-permute-start(bf16[1,512,3,256]{3,1,2,0:T(8,128)(2,1)} %convert_element_type.61), channel_id=1, source_target_pairs={{16,0},{32,16},{48,32},{64,48},{80,64},{96,80},{112,96},{128,112},... | collective-permute-start | bytes 2359304 | tf_op jit(solution)/shard_map/ppermute | solution.py:18
  445.5 3.0 copy-start.4
  454.7 4.8 copy-start.5
  459.5 4.5 copy-start.10
  464.0 3.6 copy-start.9
  467.6 2.2 copy-start.8
  469.8 2.2 copy-start.7
  469.8 2.2 copy-start.11
  472.0 254.5 %copy-start.1 = (bf16[1,128,8192]{2,1,0:T(8,128)(2,1)S(1)}, bf16[1,128,8192]{2,1,0:T(8,128)(2,1)}, u32[]{:S(2)}) copy-start(bf16[1,128,8192]{2,1,0:T(8,128)(2,1)} %param.8) | copy-start | bytes 6291460
Sparse Core Ops, SparseCore 0:
  21.7 270.2 all-gather.6
  293.8 67.7 all-gather.10
  363.3 80.5 all-gather.8
  446.3 277.4 reduce-scatter.1
where the time goes:
time: 733 us
  waiting for transfers between devices  645 us (88%)
  matrix products  33.5 us (5%)
  other arithmetic  21.3 us (3%)
  local copies, waits for them, and re-layouts  14.1 us (2%)
  between operations  14.1 us (2%)
    all_gather x1, waiting for transfers between devices, shards(): shard_piece = lax.all_gather(weights, 'seq', axis=0, tiled=True)  266 us
    reduce_scatter x1, waiting for transfers between devices, shards(): lax.psum_scatter(jnp.stack([token_contract(normed_part, gate_grad), token...  248 us
    all_gather x1, waiting for transfers between devices, shards(): key_piece = lax.all_gather(attn_keys[0], 'seq', axis=0, tiled=True)  76.6 us
    all_gather x1, waiting for transfers between devices, shards(): value_piece = lax.all_gather(attn_values[0], 'seq', axis=0, tiled=True)  45 us
  transfers between devices with their start and end apart: 6, of which 5 were waited for; matrix products, arithmetic and copies ran while one was open for 9% of the time, Pallas kernels for 0%

commit v1 on v0

v1 whole, which is shorter than its diff:
```python
import jax
import jax.numpy as jnp
from jax import lax
from jax.sharding import Mesh, PartitionSpec as P

HD = 128
QH = 32
KVH = 4

EPSILON = 1e-05
NEGATIVE = -1e30


def shifted(block, axis, distance):
    devices = range(lax.axis_size(axis))
    route = [((i - distance) % len(devices), i) for i in devices]
    return lax.ppermute(block, axis, route)


def token_contract(left, right):
    return lax.dot_general(
        left, right, (((0,), (0,)), ((), ())), preferred_element_type=jnp.float32
    )


def matmul(left, right):
    return jnp.dot(left, right, preferred_element_type=jnp.float32)


def normalize(activation):
    widened = activation.astype(jnp.float32)
    factor = lax.rsqrt(jnp.mean(widened * widened, axis=-1, keepdims=True) + EPSILON)
    return (widened * factor).astype(jnp.bfloat16)


def swiglu_back(gate_sum, up_sum, hidden_grad):
    sigmoid_gate = jax.nn.sigmoid(gate_sum)
    activated = gate_sum * sigmoid_gate
    hidden = (activated * up_sum).astype(jnp.bfloat16)
    up_grad = (hidden_grad * activated).astype(jnp.bfloat16)
    gate_grad = (
        hidden_grad * up_sum * sigmoid_gate * (1.0 + gate_sum * (1.0 - sigmoid_gate))
    ).astype(jnp.bfloat16)
    return (hidden, gate_grad, up_grad)


def pair_split(block, side):
    rows, columns = block.shape
    halves = block.reshape(rows, 2, columns // 2)
    first = side == 0
    keep = jnp.where(first, halves[:, 0], halves[:, 1])
    give = jnp.where(first, halves[:, 1], halves[:, 0])
    return keep, give


def pair_rows(own, other, side):
    first = side == 0
    return jnp.concatenate([jnp.where(first, own, other), jnp.where(first, other, own)], axis=0)


def feature_split(block, side, layers):
    rows, columns = block.shape
    pieces = block.reshape(rows, layers, 2, columns // layers // 2)
    first = side == 0
    keep = jnp.where(first, pieces[:, :, 0], pieces[:, :, 1]).reshape(rows, columns // 2)
    give = jnp.where(first, pieces[:, :, 1], pieces[:, :, 0]).reshape(rows, columns // 2)
    return keep, give


def attend(queries, keys, values, first_row):
    rows, columns = queries.shape
    kv_heads = keys.shape[1] // HD
    group = columns // HD // kv_heads
    length = keys.shape[0]
    grouped = queries.reshape(rows, kv_heads, group, HD)
    query_pos = first_row + jnp.arange(rows, dtype=jnp.int32)
    running_max = jnp.full((kv_heads, group, rows), NEGATIVE, jnp.float32)
    running_sum = jnp.zeros((kv_heads, group, rows), jnp.float32)
    summed = jnp.zeros((kv_heads, group, rows, HD), jnp.float32)
    block_rows = min(512, length)
    for offset in range(0, length, block_rows):
        key_block = keys[offset : offset + block_rows].reshape(block_rows, kv_heads, HD)
        value_block = values[offset : offset + block_rows].reshape(block_rows, kv_heads, HD)
        scores = jnp.einsum(
            "skgd,pkd->kgsp", grouped, key_block, preferred_element_type=jnp.float32
        ) * HD ** (-0.5)
        key_pos = offset + jnp.arange(block_rows, dtype=jnp.int32)
        allowed = key_pos[None, :] <= query_pos[:, None]
        scores = jnp.where(allowed, scores, NEGATIVE)
        new_max = jnp.maximum(running_max, jnp.max(scores, axis=-1))
        probs = jnp.where(allowed, jnp.exp(scores - new_max[..., None]), 0.0)
        rescale = jnp.exp(running_max - new_max)
        running_sum = running_sum * rescale + jnp.sum(probs, axis=-1)
        summed = summed * rescale[..., None] + jnp.einsum(
            "kgsp,pkd->kgsd",
            probs.astype(jnp.bfloat16),
            value_block,
            preferred_element_type=jnp.float32,
        )
        running_max = new_max
    result = summed / running_sum[..., None]
    return jnp.transpose(result, (2, 0, 1, 3)).reshape(rows, columns).astype(jnp.bfloat16)


def shards(saved_input, output_grad, weight_span, grad_carry, attn_queries, attn_keys, attn_values):
    side = lax.axis_index("x")
    layer = lax.axis_index("z")
    layers = lax.axis_size("z")
    rows = saved_input.shape[1]

    key_keep, key_give = pair_split(attn_keys[0], side)
    value_keep, value_give = pair_split(attn_values[0], side)
    pair_keep = jnp.concatenate([key_keep, value_keep], axis=1)
    pair_give = jnp.concatenate([key_give, value_give], axis=1)
    pair_got = shifted(pair_give, "x", 1)
    arrived = shifted(jnp.transpose(weight_span[0], (1, 0, 2)), "blk", 1)
    keys_values = lax.all_gather(pair_rows(pair_keep, pair_got, side), "z", axis=0, tiled=True)
    weights = lax.all_gather(arrived, "z", axis=1, tiled=True)

    normed_keep, normed_give = feature_split(normalize(saved_input[0]), side, layers)
    grad_keep, grad_give = feature_split(output_grad[0], side, layers)
    normed = pair_rows(normed_keep, shifted(normed_give, "x", 1), side)
    cotangent = pair_rows(grad_keep, shifted(grad_give, "x", 1), side)

    query_keep, query_give = pair_split(attn_queries[0], side)
    queries = pair_rows(query_keep, shifted(query_give, "x", 1), side)
    carried = shifted(jnp.transpose(grad_carry[0], (1, 0, 2)).astype(jnp.bfloat16), "blk", -1)

    partial = jnp.stack(
        [matmul(normed, weights[0]), matmul(normed, weights[1]), matmul(cotangent, weights[2])]
    )
    sums = partial + shifted(partial.astype(jnp.bfloat16), "x", 1).astype(jnp.float32)
    hidden, gate_grad, up_grad = swiglu_back(sums[0], sums[1], sums[2])
    update = jnp.stack(
        [
            token_contract(normed, gate_grad),
            token_contract(normed, up_grad),
            token_contract(cotangent, hidden),
        ]
    ).astype(jnp.bfloat16)
    update = lax.psum_scatter(update, "z", scatter_dimension=1, tiled=True)
    carry_out = carried.astype(jnp.float32) + update.astype(jnp.float32)
    carry_out = jnp.transpose(carry_out, (1, 0, 2))[None]

    half = keys_values.shape[1] // 2
    both = attend(queries, keys_values[:, :half], keys_values[:, half:], layer * 2 * rows)
    first = side == 0
    mine = jnp.where(first, both[:rows], both[rows:])
    theirs = jnp.where(first, both[rows:], both[:rows])
    got = shifted(theirs, "x", 1)
    attn_out = jnp.concatenate([jnp.where(first, mine, got), jnp.where(first, got, mine)], axis=1)
    return (carry_out, attn_out[None])


def solution(mesh):
    workers, parts = mesh.devices.shape
    split = Mesh(mesh.devices.reshape(workers, parts // 2, 2), ("blk", "z", "x"))
    seq = ("z", "x")
    return jax.shard_map(
        shards,
        mesh=split,
        in_specs=(
            P("blk", seq, None),
            P("blk", seq, None),
            P("blk", seq, None, None),
            P("blk", seq, None, None),
            P("blk", seq, None),
            P("blk", seq, None),
            P("blk", seq, None),
        ),
        out_specs=(P("blk", seq, None, None), P("blk", seq, None)),
        check_vma=False,
    )
```

time: 733 us -> 233 us (0.32)
  waiting for transfers between devices: 645 us -> 144 us
  matrix products: 33.5 us -> 22.2 us
  starting transfers between devices: 5.03 us -> 14.9 us
    all_gather x3 -> x2, waiting for transfers between devices: 387 us -> 30.2 us  [the longest x1 22.7 us: shards(): weights = lax.all_gather(arrived, 'z', axis=1, tiled=True)]
    reduce_scatter x1, waiting for transfers between devices: 248 us -> 30.4 us  [shards(): update = lax.psum_scatter(update, 'z', scatter_dimension=1, tiled=True)]
    ppermute x2 -> x8, waiting for transfers between devices: 9.25 us -> 83.7 us  [shifted(): return lax.ppermute(block, axis, route)]
    ppermute x2 -> x8, starting transfers between devices: 4.87 us -> 14.7 us  [shifted(): return lax.ppermute(block, axis, route)]
  transfers between devices with their start and end apart: 6 -> 11, of which waited for: 5 -> 9; matrix products, arithmetic and copies ran while one was open for 9% -> 23% of each run, Pallas kernels for 0% -> 0%
where the time goes in v1:
time: 233 us
  waiting for transfers between devices  144 us (62%)
  other arithmetic  23.3 us (10%)
  matrix products  22.2 us (10%)
  starting transfers between devices  14.9 us (6%)
  local copies, waits for them, and re-layouts  14.2 us (6%)
  between operations  14.1 us (6%)
    ppermute x8, waiting for transfers between devices, shifted(): return lax.ppermute(block, axis, route)  83.7 us
    reduce_scatter x1, waiting for transfers between devices, shards(): update = lax.psum_scatter(update, 'z', scatter_dimension=1, tiled=True)  30.4 us
    all_gather x1, waiting for transfers between devices, shards(): weights = lax.all_gather(arrived, 'z', axis=1, tiled=True)  22.7 us
    ppermute x8, starting transfers between devices, shifted(): return lax.ppermute(block, axis, route)  14.7 us
    unnamed x24, local copies, waits for them, and re-layouts  12.4 us
    dot_general x4, matrix products, attend(): jnp.einsum('kgsp,pkd->kgsd', probs.astype(jnp.bfloat16), value_block, pre...  9.74 us
    reduce_sum x4, other arithmetic, attend(): running_sum = running_sum * rescale + jnp.sum(probs, axis=-1)  8.24 us
    all_gather x1, waiting for transfers between devices, shards(): lax.all_gather(pair_rows(pair_keep, pair_got, side), 'z', axis=0, tiled=T...  7.5 us
  transfers between devices with their start and end apart: 11, of which 9 were waited for; matrix products, arithmetic and copies ran while one was open for 23% of the time, Pallas kernels for 0%

profile of v1, /device:TPU:1, one launch (start us, length us, event | category | flops | bytes accessed | tf_op | source)
XLA Modules:
  0.0 233.1 jit_solution(3044764760419843513)
XLA Ops:
  7.2 4.2 %collective-permute-start.2 = (bf16[3,512,256]{2,1,0:T(8,128)(2,1)}, bf16[3,512,256]{2,1,0:T(8,128)(2,1)S(1)}, u32[]{:S(2)}, u32[]{:S(2)}) collective-permute-start(bf16[3,512,256]{2,1,0:T(8,128)(2,1)} %bitcast.307), channel_id=1, source_target_pairs={{240,0},{0,16},{16,32},{32,48},{48,64},{64,80},{80,96},{96,112},{1... | collective-permute-start | bytes 2359304 | tf_op jit(solution)/shard_map/ppermute | solution.py:17
  11.4 9.3 %collective-permute-done.2 = bf16[3,512,256]{2,1,0:T(8,128)(2,1)S(1)} collective-permute-done((bf16[3,512,256]{2,1,0:T(8,128)(2,1)}, bf16[3,512,256]{2,1,0:T(8,128)(2,1)S(1)}, u32[]{:S(2)}, u32[]{:S(2)}) %collective-permute-start.2) | collective-permute-done | bytes 786464 | tf_op jit(solution)/shard_map/ppermute | solution.py:17
  21.6 3.2 %copy.36 = bf16[1,128,8192]{1,2,0:T(8,128)(2,1)S(1)} copy(bf16[1,128,8192]{2,1,0:T(8,128)(2,1)} %param.7) | data formatting | bytes 4194304 | tf_op args[0]
  28.0 3.2 %copy.37 = bf16[1,128,8192]{1,2,0:T(8,128)(2,1)S(1)} copy(bf16[1,128,8192]{2,1,0:T(8,128)(2,1)} %param.8) | data formatting | bytes 4194304 | tf_op args[1]
  34.6 38.3 %collective-permute-done.5 = bf16[128,512]{0,1:T(8,128)(2,1)S(1)} collective-permute-done((bf16[128,512]{0,1:T(8,128)(2,1)S(1)}, bf16[128,512]{0,1:T(8,128)(2,1)S(1)}, u32[]{:S(2)}, u32[]{:S(2)}) %collective-permute-start.5) | collective-permute-done | bytes 131104 | tf_op jit(solution)/shard_map/ppermute | solution.py:17
  73.7 3.4 %bitcast_select_fusion.5 = (bf16[128,4096]{0,1:T(8,128)(2,1)}, bf16[128,4096]{0,1:T(8,128)(2,1)}, bf16[128,4096]{0,1:T(8,128)(2,1)S(1)}, bf16[128,4096]{0,1:T(8,128)(2,1)}) fusion(bf16[128,4096]{0,1:T(8,128)(2,1)S(1)} %collective-permute-done.3, bf16[128,8,1,512]{0,3,2,1:T(8,128)(2,1)} %get-tuple-element.26, pred[]{:T(512)S(6)} %eq.2, ...), kind=kLoop, calls=%fused_computation.61 | loop fusion | flops 2097152 | bytes 8388609 | tf_op jit(solution)/shard_map/jit(_where)/select_n | solution.py:58
  77.1 22.7 %all-gather.3.cloned.1.call-done = bf16[3,4096,256]{2,1,0:T(8,128)(2,1)} async-done(((bf16[3,512,256]{2,1,0:T(8,128)(2,1)}), bf16[3,4096,256]{2,1,0:T(8,128)(2,1)}) %all-gather.3.cloned.1.call-update) | async-done | bytes 6291472 | tf_op jit(solution)/shard_map/all_gather | solution.py:118
  99.8 2.8 %fusion.37 = f32[1,256,256]{2,1,0:T(8,128)S(1)} fusion(bf16[3,4096,256]{2,1,0:T(8,128)(2,1)} %all-gather.3.cloned.1.call-done, bf16[128,4096]{0,1:T(8,128)(2,1)S(1)} %get-tuple-element.55, bf16[128,4096]{0,1:T(8,128)(2,1)} %get-tuple-element.56), kind=kOutput, calls=%fused_computation.55 | convolution fusion | flops 541065216 | bytes 4456448 | tf_op jit(solution)/shard_map/dot_general | solution.py:27
  107.2 8.9 %collective-permute-done.4 = bf16[3,256,256]{2,1,0:T(8,128)(2,1)S(1)} collective-permute-done((bf16[3,256,256]{2,1,0:T(8,128)(2,1)S(1)}, bf16[3,256,256]{2,1,0:T(8,128)(2,1)S(1)}, u32[]{:S(2)}, u32[]{:S(2)}) %collective-permute-start.4) | collective-permute-done | bytes 393248 | tf_op jit(solution)/shard_map/ppermute | solution.py:17
  118.5 3.1 %pad_maximum_fusion = bf16[3,4096,256]{2,1,0:T(8,128)(2,1)} fusion(bf16[1,4096,256]{2,1,0:T(8,128)(2,1)S(1)} %fusion.14, bf16[1,4096,256]{2,1,0:T(8,128)(2,1)S(1)} %fusion.13, bf16[1,4096,256]{2,1,0:T(8,128)(2,1)S(1)} %fusion.12), kind=kLoop, calls=%fused_computation.12 | loop fusion | flops 6291456 | bytes 12582912 | tf_op jit(solution)/shard_map/stack | solution.py:134
  125.4 10.5 %collective-permute-done.6 = bf16[128,2048]{0,1:T(8,128)(2,1)S(1)} collective-permute-done((bf16[128,2048]{0,1:T(8,128)(2,1)S(1)}, bf16[128,2048]{0,1:T(8,128)(2,1)S(1)}, u32[]{:S(2)}, u32[]{:S(2)}) %collective-permute-start.6) | collective-permute-done | bytes 524320 | tf_op jit(solution)/shard_map/ppermute | solution.py:17
  136.1 7.5 %all-gather.5.cloned.1.call-done = bf16[2048,512]{0,1:T(8,128)(2,1)} async-done(((bf16[256,512]{0,1:T(8,128)(2,1)}), bf16[2048,512]{0,1:T(8,128)(2,1)}) %all-gather.5.cloned.1.call-update) | async-done | bytes 2097168 | tf_op jit(solution)/shard_map/all_gather | solution.py:117
  151.3 2.2 fusion.4
  155.5 2.0 fusion.8
  157.5 2.0 fusion.10
  159.6 2.3 %fusion.19 = f32[2,8,256,128]{2,3,1,0:T(8,128)S(1)} fusion(bf16[512,2,128,1]{0,2,3,1:T(8,128)(2,1)S(1)} %bitcast.306, f32[2,512,256,8]{2,1,3,0:T(8,128)S(1)} %get-tuple-element.52, f32[2,8,256]{2,1,0:T(8,128)S(1)} %get-tuple-element.11, pred[256,512]{0,1:T(8,128)(4,1)S(1)} %get-tuple-element.44), kind=kOutput, calls=%fused_computation.31 | convolution fusion | flops 547356672 | bytes 10895360 | tf_op jit(solution)/shard_map/kgsp,pkd->kgsd/dot_general | solution.py:94
  161.9 2.3 %fusion.17 = f32[2,8,256,128]{2,3,1,0:T(8,128)S(1)} fusion(bf16[512,2,128,1]{0,2,3,1:T(8,128)(2,1)S(1)} %bitcast.305, f32[2,512,256,8]{2,1,3,0:T(8,128)S(1)} %get-tuple-element.50, f32[2,8,256]{2,1,0:T(8,128)S(1)} %get-tuple-element.10, pred[256,512]{0,1:T(8,128)(4,1)S(1)} %get-tuple-element.45), kind=kOutput, calls=%fused_computation.30 | convolution fusion | flops 547356672 | bytes 10895360 | tf_op jit(solution)/shard_map/kgsp,pkd->kgsd/dot_general | solution.py:94
  164.3 2.3 %fusion.15 = f32[2,8,256,128]{2,3,1,0:T(8,128)S(1)} fusion(bf16[512,2,128,1]{0,2,3,1:T(8,128)(2,1)S(1)} %bitcast.304, f32[2,512,256,8]{2,1,3,0:T(8,128)S(1)} %get-tuple-element.48, f32[2,8,256]{2,1,0:T(8,128)S(1)} %get-tuple-element.9, pred[256,512]{0,1:T(8,128)(4,1)S(1)} %get-tuple-element.46), kind=kOutput, calls=%fused_computation.29 | convolution fusion | flops 547356672 | bytes 10895360 | tf_op jit(solution)/shard_map/kgsp,pkd->kgsd/dot_general | solution.py:94
  166.6 2.7 %fusion.31 = bf16[256,2,8,128]{0,3,2,1:T(8,128)(2,1)S(1)} fusion(f32[2,8,256,128]{2,3,1,0:T(8,128)S(1)} %fusion.15, f32[2,8,256,128]{2,3,1,0:T(8,128)S(1)} %fusion.17, f32[2,8,256,128]{2,3,1,0:T(8,128)S(1)} %fusion.19, bf16[512,2,128,1]{0,2,3,1:T(8,128)(2,1)S(1)} %bitcast.303, f32[2,512,256,8]{2,1,3,0:T(8,128)S(1)} %get-tuple-element.54, ...), kind=kOutput, calls=%fused_computation.47 | convolution fusion | flops 552075264 | bytes 16220160 | tf_op jit(solution)/shard_map/kgsp,pkd->kgsd/dot_general | solution.py:94
  170.8 4.6 %collective-permute-start = (bf16[3,512,256]{2,1,0:T(8,128)(2,1)S(1)}, bf16[3,512,256]{2,1,0:T(8,128)(2,1)S(1)}, u32[]{:S(2)}, u32[]{:S(2)}) collective-permute-start(bf16[3,512,256]{2,1,0:T(8,128)(2,1)S(1)} %convert_bitcast_fusion), channel_id=1, source_target_pairs={{16,0},{32,16},{48,32},{64,48},{80,64},{96,80},{112,96},{128,112},... | collective-permute-start | bytes 2359304 | tf_op jit(solution)/shard_map/ppermute | solution.py:17
  175.4 2.7 %collective-permute-done.7 = bf16[128,2048]{0,1:T(8,128)(2,1)S(1)} collective-permute-done((bf16[128,2048]{0,1:T(8,128)(2,1)S(1)}, bf16[128,2048]{0,1:T(8,128)(2,1)S(1)}, u32[]{:S(2)}, u32[]{:S(2)}) %collective-permute-start.7) | collective-permute-done | bytes 524320 | tf_op jit(solution)/shard_map/ppermute | solution.py:17
  179.5 14.2 %collective-permute-done = bf16[3,512,256]{2,1,0:T(8,128)(2,1)S(1)} collective-permute-done((bf16[3,512,256]{2,1,0:T(8,128)(2,1)S(1)}, bf16[3,512,256]{2,1,0:T(8,128)(2,1)S(1)}, u32[]{:S(2)}, u32[]{:S(2)}) %collective-permute-start) | collective-permute-done | bytes 786464 | tf_op jit(solution)/shard_map/ppermute | solution.py:17
  193.7 30.4 %reduce-scatter.2.cloned.1.call-done = bf16[3,512,256]{2,1,0:T(8,128)(2,1)} async-done(((bf16[3,4096,256]{2,1,0:T(8,128)(2,1)}), bf16[3,512,256]{2,1,0:T(8,128)(2,1)}) %reduce-scatter.2.cloned.1.call-update) | async-done | bytes 786448 | tf_op jit(solution)/shard_map/reduce_scatter | solution.py:141
  224.1 2.4 %add_bitcast_fusion = f32[1,512,3,256]{3,1,2,0:T(8,128)} fusion(bf16[3,512,256]{2,1,0:T(8,128)(2,1)} %reduce-scatter.2.cloned.1.call-done, bf16[3,512,256]{2,1,0:T(8,128)(2,1)S(1)} %collective-permute-done), kind=kLoop, calls=%fused_computation.54 | loop fusion | flops 1179648 | bytes 3145728 | tf_op jit(solution)/shard_map/broadcast_in_dim | solution.py:143
  (71 shorter events, 31.8 us)
Async XLA Ops:
  7.2 92.6 %all-gather.3.cloned.1.call-start = ((), (), s32[]{:S(2)}) async-start(), calls=%async_computation.1 | async-start | bytes 7077888 | tf_op jit(solution)/shard_map/all_gather | solution.py:118
  7.2 13.5 %collective-permute-start.2 = (bf16[3,512,256]{2,1,0:T(8,128)(2,1)}, bf16[3,512,256]{2,1,0:T(8,128)(2,1)S(1)}, u32[]{:S(2)}, u32[]{:S(2)}) collective-permute-start(bf16[3,512,256]{2,1,0:T(8,128)(2,1)} %bitcast.307), channel_id=1, source_target_pairs={{240,0},{0,16},{16,32},{32,48},{48,64},{64,80},{80,96},{96,112},{1... | collective-permute-start | bytes 2359304 | tf_op jit(solution)/shard_map/ppermute | solution.py:17
  20.7 0.9 copy-start.5
  21.6 122.0 %all-gather.5.cloned.1.call-start = ((), (), s32[]{:S(2)}) async-start(), calls=%async_computation.3 | async-start | bytes 2359296 | tf_op jit(solution)/shard_map/all_gather | solution.py:117
  27.7 6.2 %copy-start.6 = (bf16[1,128,512]{2,1,0:T(8,128)(2,1)S(1)}, bf16[1,128,512]{2,1,0:T(8,128)(2,1)}, u32[]{:S(2)}) copy-start(bf16[1,128,512]{2,1,0:T(8,128)(2,1)} %param.12) | copy-start | bytes 393220
  27.7 6.3 %copy-start.7 = (bf16[1,128,512]{2,1,0:T(8,128)(2,1)S(1)}, bf16[1,128,512]{2,1,0:T(8,128)(2,1)}, u32[]{:S(2)}) copy-start(bf16[1,128,512]{2,1,0:T(8,128)(2,1)} %param.13) | copy-start | bytes 393220
  27.7 46.0 %collective-permute-start.1 = (bf16[128,4096]{0,1:T(8,128)(2,1)}, bf16[128,4096]{0,1:T(8,128)(2,1)}, u32[]{:S(2)}, u32[]{:S(2)}) collective-permute-start(bf16[128,4096]{0,1:T(8,128)(2,1)} %bitcast.4), channel_id=1, source_target_pairs={{1,0},{0,1},{3,2},{2,3},{5,4},{4,5},{7,6},{6,7},{9,8},{8,9},{11,10... | collective-permute-start | bytes 3145736 | tf_op jit(solution)/shard_map/ppermute | solution.py:17
  32.7 41.0 %collective-permute-start.3 = (bf16[128,4096]{0,1:T(8,128)(2,1)}, bf16[128,4096]{0,1:T(8,128)(2,1)S(1)}, u32[]{:S(2)}, u32[]{:S(2)}) collective-permute-start(bf16[128,4096]{0,1:T(8,128)(2,1)} %bitcast.13), channel_id=1, source_target_pairs={{1,0},{0,1},{3,2},{2,3},{5,4},{4,5},{7,6},{6,7},{9,8},{8,9},{11,10... | collective-permute-start | bytes 3145736 | tf_op jit(solution)/shard_map/ppermute | solution.py:17
  34.1 38.7 %collective-permute-start.5 = (bf16[128,512]{0,1:T(8,128)(2,1)S(1)}, bf16[128,512]{0,1:T(8,128)(2,1)S(1)}, u32[]{:S(2)}, u32[]{:S(2)}) collective-permute-start(bf16[128,512]{0,1:T(8,128)(2,1)S(1)} %pad_maximum_fusion.11), channel_id=1, source_target_pairs={{1,0},{0,1},{3,2},{2,3},{5,4},{4,5},{7,6},{6,7},{9,8},{8,9},{11,10... | collective-permute-start | bytes 393224 | tf_op jit(solution)/shard_map/ppermute | solution.py:17
  73.6 150.5 %reduce-scatter.2.cloned.1.call-start = ((), (), s32[]{:S(2)}) async-start(), calls=%async_computation.2 | async-start | bytes 7077888 | tf_op jit(solution)/shard_map/reduce_scatter | solution.py:141
  77.1 25.5 %copy-start.1 = (bf16[128,4096]{0,1:T(8,128)(2,1)S(1)}, bf16[128,4096]{0,1:T(8,128)(2,1)}, u32[]{:S(2)}) copy-start(bf16[128,4096]{0,1:T(8,128)(2,1)} %get-tuple-element.56) | copy-start | bytes 3145732
  99.8 3.7 %copy-start.8 = (bf16[3,4096,256]{2,1,0:T(8,128)(2,1)S(1)}, bf16[3,4096,256]{2,1,0:T(8,128)(2,1)}, u32[]{:S(2)}) copy-start(bf16[3,4096,256]{2,1,0:T(8,128)(2,1)} %all-gather.3.cloned.1.call-done) | copy-start | bytes 18874372
  103.5 1.2 copy-start.2
  103.5 1.5 copy-start.3
  105.9 10.2 %collective-permute-start.4 = (bf16[3,256,256]{2,1,0:T(8,128)(2,1)S(1)}, bf16[3,256,256]{2,1,0:T(8,128)(2,1)S(1)}, u32[]{:S(2)}, u32[]{:S(2)}) collective-permute-start(bf16[3,256,256]{2,1,0:T(8,128)(2,1)S(1)} %fusion.40), channel_id=1, source_target_pairs={{1,0},{0,1},{3,2},{2,3},{5,4},{4,5},{7,6},{6,7},{9,8},{8,9},{11,10... | collective-permute-start | bytes 1179656 | tf_op jit(solution)/shard_map/ppermute | solution.py:17
  121.6 1.2 copy-start.4
  123.5 12.3 %collective-permute-start.6 = (bf16[128,2048]{0,1:T(8,128)(2,1)S(1)}, bf16[128,2048]{0,1:T(8,128)(2,1)S(1)}, u32[]{:S(2)}, u32[]{:S(2)}) collective-permute-start(bf16[128,2048]{0,1:T(8,128)(2,1)S(1)} %select_bitcast_fusion), channel_id=1, source_target_pairs={{1,0},{0,1},{3,2},{2,3},{5,4},{4,5},{7,6},{6,7},{9,8},{8,9},{11,10... | collective-permute-start | bytes 1572872 | tf_op jit(solution)/shard_map/ppermute | solution.py:17
  166.6 4.1 %copy-start = (f32[1,512,3,256]{3,1,2,0:T(8,128)S(1)}, f32[1,512,3,256]{3,1,2,0:T(8,128)}, u32[]{:S(2)}) copy-start(f32[1,512,3,256]{3,1,2,0:T(8,128)} %param.10) | copy-start | bytes 4718596
  169.5 8.6 %collective-permute-start.7 = (bf16[128,2048]{0,1:T(8,128)(2,1)S(1)}, bf16[128,2048]{0,1:T(8,128)(2,1)S(1)}, u32[]{:S(2)}, u32[]{:S(2)}) collective-permute-start(bf16[128,2048]{0,1:T(8,128)(2,1)S(1)} %bitcast.300), channel_id=1, source_target_pairs={{1,0},{0,1},{3,2},{2,3},{5,4},{4,5},{7,6},{6,7},{9,8},{8,9},{11,10... | collective-permute-start | bytes 1572872 | tf_op jit(solution)/shard_map/ppermute | solution.py:17
  170.8 22.9 %collective-permute-start = (bf16[3,512,256]{2,1,0:T(8,128)(2,1)S(1)}, bf16[3,512,256]{2,1,0:T(8,128)(2,1)S(1)}, u32[]{:S(2)}, u32[]{:S(2)}) collective-permute-start(bf16[3,512,256]{2,1,0:T(8,128)(2,1)S(1)} %convert_bitcast_fusion), channel_id=1, source_target_pairs={{16,0},{32,16},{48,32},{64,48},{80,64},{96,80},{112,96},{128,112},... | collective-permute-start | bytes 2359304 | tf_op jit(solution)/shard_map/ppermute | solution.py:17
Sparse Core Ops, SparseCore 0:
  21.7 78.0 all-gather.2
  101.5 42.0 all-gather.4
  146.2 77.9 reduce-scatter.1
